TPU v7x, 32 devices: a whole 2x2x4 slice. The times are simulated.
32 devices in a mesh: corner: 8 (over y, x, core), tm: 4 (over z).
Axes of the slice: x: 2, y: 2, z: 4, core: 2. Of those that a mesh axis runs over, the one named last changes fastest.
Arguments:
- signal: bfloat16 [8, 64, 16384], P('corner', None, 'tm'), may hold values from -6 to 6
- dilated_conv_weight: bfloat16 [2, 256, 128], replicated, may hold values from -0.5 to 0.5
- dilated_conv_bias: float32 [2, 256], replicated, may hold values from -3 to 3
- projection_weight: bfloat16 [2, 128, 128], replicated, may hold values from -0.5 to 0.5
- projection_bias: float32 [2, 128], replicated, may hold values from -3 to 3
- cot_top: bfloat16 [8, 64, 16384], P('corner', None, 'tm'), may hold values from -6 to 6
- cot_skip: bfloat16 [8, 64, 16384], P('corner', None, 'tm'), may hold values from -6 to 6
Outputs:
- x_top: bfloat16 [8, 64, 16384], P('corner', None, 'tm')
- skip_sum: bfloat16 [8, 64, 16384], P('corner', None, 'tm')
- grad_input: bfloat16 [8, 64, 16384], P('corner', None, 'tm')
- grad_conv: float32 [2, 256, 128], replicated
- grad_conv_bias: float32 [2, 256], replicated
- grad_out: float32 [2, 128, 128], replicated
- grad_out_bias: float32 [2, 128], replicated
All inputs are finite; a program needn't handle non-finite values.
Results may differ from a plain program's by a relative error of at most 0.0065.
Values may be sent and summed in bfloat16 or wider, within the bound.
A program may use at most 64 MiB of HBM per device.

v0:
```python
import math

import jax
import jax.numpy as jnp
from jax import lax
from jax.sharding import PartitionSpec as P


def from_behind(block, axis, distance):
    devices = range(lax.axis_size(axis))
    route = [(i - distance, i) for i in devices if i - distance in devices]
    return lax.ppermute(block, axis, route)


def gated_layer_forward(a_in, tap_in, weight, bias, proj, proj_bias, gsize, rsize):
    stacked = jnp.concatenate([tap_in, a_in], axis=1)
    pre_act = (
        jnp.einsum("oc,bct->bot", weight, stacked, preferred_element_type=jnp.float32)
        + bias[None, :, None]
    )
    gate_out = (jnp.tanh(pre_act[:, :gsize]) * jax.nn.sigmoid(pre_act[:, gsize:])).astype(
        jnp.bfloat16
    )
    mixed = (
        jnp.einsum("og,bgt->bot", proj, gate_out, preferred_element_type=jnp.float32)
        + proj_bias[None, :, None]
    )
    next_act = (a_in.astype(jnp.float32) + mixed[:, :rsize]).astype(jnp.bfloat16)
    return (stacked, pre_act, gate_out, next_act, mixed[:, rsize:])


def layer_backward(go_res, go_skip, stacked, pre_act, gate_out, weight, proj, gsize, rsize):
    upper = jnp.concatenate([go_res, go_skip], axis=1)
    grad_proj = jnp.einsum("bot,bgt->og", upper, gate_out, preferred_element_type=jnp.float32)
    grad_pbias = jnp.sum(upper, axis=(0, 2), dtype=jnp.float32)
    grad_gate = jnp.einsum("og,bot->bgt", proj, upper, preferred_element_type=jnp.float32)
    filt_act = jnp.tanh(pre_act[:, :gsize])
    gate_act = jax.nn.sigmoid(pre_act[:, gsize:])
    grad_pre = jnp.concatenate(
        [
            grad_gate * gate_act * (1.0 - filt_act * filt_act),
            grad_gate * filt_act * gate_act * (1.0 - gate_act),
        ],
        axis=1,
    ).astype(jnp.bfloat16)
    grad_weight = jnp.einsum("bot,bct->oc", grad_pre, stacked, preferred_element_type=jnp.float32)
    grad_bias = jnp.sum(grad_pre, axis=(0, 2), dtype=jnp.float32)
    grad_in = jnp.einsum("oc,bot->bct", weight, grad_pre, preferred_element_type=jnp.float32)
    return (
        grad_in[:, :rsize].astype(jnp.bfloat16),
        grad_in[:, rsize:],
        (grad_weight, grad_bias, grad_proj, grad_pbias),
    )


def on_device(
    signal,
    dilated_conv_weight,
    dilated_conv_bias,
    projection_weight,
    projection_bias,
    cot_top,
    cot_skip,
):
    rsize = signal.shape[1]
    gsize = projection_weight.shape[2]
    tap_near = from_behind(signal, "tm", 1)
    (
        lower_saved_state,
        lower_preactivation,
        lower_gated_output,
        middle_layer_input,
        lower_skip_output,
    ) = gated_layer_forward(
        signal,
        tap_near,
        dilated_conv_weight[0],
        dilated_conv_bias[0],
        projection_weight[0],
        projection_bias[0],
        gsize,
        rsize,
    )
    tap_far = from_behind(middle_layer_input, "tm", 2)
    (
        upper_saved_state,
        upper_preactivation,
        upper_gated_output,
        upper_layer_output,
        upper_skip_output,
    ) = gated_layer_forward(
        middle_layer_input,
        tap_far,
        dilated_conv_weight[1],
        dilated_conv_bias[1],
        projection_weight[1],
        projection_bias[1],
        gsize,
        rsize,
    )
    skip_out = (lower_skip_output + upper_skip_output).astype(jnp.bfloat16)
    delayed_gradient_upper, current_gradient_upper, grads_top = layer_backward(
        cot_top,
        cot_skip,
        upper_saved_state,
        upper_preactivation,
        upper_gated_output,
        dilated_conv_weight[1],
        projection_weight[1],
        gsize,
        rsize,
    )
    later_top = from_behind(delayed_gradient_upper, "tm", -2)
    middle_input_gradient = (
        cot_top.astype(jnp.float32) + current_gradient_upper + later_top.astype(jnp.float32)
    ).astype(jnp.bfloat16)
    delayed_gradient_lower, current_gradient_lower, grads_low = layer_backward(
        middle_input_gradient,
        cot_skip,
        lower_saved_state,
        lower_preactivation,
        lower_gated_output,
        dilated_conv_weight[0],
        projection_weight[0],
        gsize,
        rsize,
    )
    later_low = from_behind(delayed_gradient_lower, "tm", -1)
    lower_input_gradient = (
        middle_input_gradient.astype(jnp.float32)
        + current_gradient_lower
        + later_low.astype(jnp.float32)
    ).astype(jnp.bfloat16)
    summed = lax.psum(
        (
            jnp.stack([grads_low[0], grads_top[0]]),
            jnp.stack([grads_low[1], grads_top[1]]),
            jnp.stack([grads_low[2], grads_top[2]]),
            jnp.stack([grads_low[3], grads_top[3]]),
        ),
        ("corner", "tm"),
    )
    count = signal.shape[0] * lax.axis_size("corner") * signal.shape[2] * lax.axis_size("tm")
    scale = 1.0 / math.sqrt(count)
    return (
        upper_layer_output,
        skip_out,
        lower_input_gradient,
        summed[0] * scale,
        summed[1] * scale,
        summed[2] * scale,
        summed[3] * scale,
    )


def solution(mesh):
    return jax.shard_map(
        on_device,
        mesh=mesh,
        in_specs=(
            P("corner", None, "tm"),
            P(),
            P(),
            P(),
            P(),
            P("corner", None, "tm"),
            P("corner", None, "tm"),
        ),
        out_specs=(
            P("corner", None, "tm"),
            P("corner", None, "tm"),
            P("corner", None, "tm"),
            P(),
            P(),
            P(),
            P(),
        ),
        check_vma=False,
    )
```

profile of v0, /device:TPU:0, one launch (start us, length us, event | category | flops | bytes accessed | tf_op | source)
XLA Modules:
  0.0 264.6 jit_solution(16260901483629337781)
XLA Ops:
  7.2 5.0 %collective-permute-start = (bf16[1,64,4096]{2,1,0:T(8,128)(2,1)}, bf16[1,64,4096]{2,1,0:T(8,128)(2,1)S(1)}, u32[]{:S(2)}, u32[]{:S(2)}) collective-permute-start(bf16[1,64,4096]{2,1,0:T(8,128)(2,1)} %param.7), channel_id=1, source_target_pairs={{0,1},{1,2},{2,3},{4,5},{5,6},{6,7},{8,9},{9,10},{10,11},{12,13},{... | collective-permute-start | bytes 1572872 | tf_op jit(solution)/shard_map/ppermute | solution.py:12
  12.2 0.8 fusion.55
  12.9 0.8 slice_bitcast_fusion
  13.7 1.1 constant_dynamic-update-slice_fusion.1
  14.8 8.8 %collective-permute-done = bf16[1,64,4096]{2,1,0:T(8,128)(2,1)S(1)} collective-permute-done((bf16[1,64,4096]{2,1,0:T(8,128)(2,1)}, bf16[1,64,4096]{2,1,0:T(8,128)(2,1)S(1)}, u32[]{:S(2)}, u32[]{:S(2)}) %collective-permute-start) | collective-permute-done | bytes 524320 | tf_op jit(solution)/shard_map/ppermute | solution.py:12
  23.6 2.0 fusion.1
  25.6 0.8 fusion.18
  26.9 0.6 copy-done.6
  27.6 5.3 %collective-permute-start.1 = (bf16[1,64,4096]{2,1,0:T(8,128)(2,1)S(1)}, bf16[1,64,4096]{2,1,0:T(8,128)(2,1)S(1)}, u32[]{:S(2)}, u32[]{:S(2)}) collective-permute-start(bf16[1,64,4096]{2,1,0:T(8,128)(2,1)S(1)} %fusion.26), channel_id=1, source_target_pairs={{0,2},{1,3},{4,6},{5,7},{8,10},{9,11},{12,14},{13,15},{16,18},{17,... | collective-permute-start | bytes 1572872 | tf_op jit(solution)/shard_map/ppermute | solution.py:12
  33.2 10.0 %collective-permute-done.1 = bf16[1,64,4096]{2,1,0:T(8,128)(2,1)S(1)} collective-permute-done((bf16[1,64,4096]{2,1,0:T(8,128)(2,1)S(1)}, bf16[1,64,4096]{2,1,0:T(8,128)(2,1)S(1)}, u32[]{:S(2)}, u32[]{:S(2)}) %collective-permute-start.1) | collective-permute-done | bytes 524320 | tf_op jit(solution)/shard_map/ppermute | solution.py:12
  43.3 0.7 fusion.3
  44.0 1.5 multiply_convert_fusion.3
  45.5 0.5 convolution_bitcast_fusion.6
  46.0 1.3 collective-permute-start.2
  47.8 1.2 fusion.24
  49.3 0.7 fusion.16
  50.1 0.4 convolution_bitcast_fusion.8
  50.5 10.4 %collective-permute-done.2 = bf16[1,64,4096]{2,1,0:T(8,128)(2,1)S(1)} collective-permute-done((bf16[1,64,4096]{2,1,0:T(8,128)(2,1)S(1)}, bf16[1,64,4096]{2,1,0:T(8,128)(2,1)S(1)}, u32[]{:S(2)}, u32[]{:S(2)}) %collective-permute-start.2) | collective-permute-done | bytes 524320 | tf_op jit(solution)/shard_map/ppermute | solution.py:12
  61.0 1.3 multiply_convert_fusion.1
  63.7 53.3 %all-reduce = (f32[2,256]{1,0:T(2,128)S(1)}, f32[2,128]{1,0:T(2,128)S(1)}) all-reduce(f32[2,256]{1,0:T(2,128)S(1)} %pad_maximum_fusion.15, f32[2,128]{1,0:T(2,128)S(1)} %pad_maximum_fusion.16), channel_id=1, replica_groups=mesh['corner'=8,'tm'=4] {'corner','tm'}, use_global_device_ids=true, to_apply=%region_3.0 | all-reduce | flops 768 | bytes 6144 | tf_op jit(solution)/shard_map/psum | solution.py:134
  117.0 0.6 broadcast_multiply_fusion.2
  117.6 2.2 convolution_bitcast_fusion.4
  119.8 0.8 slice.202
  120.6 1.3 collective-permute-start.3
  121.9 0.7 pad_maximum_fusion.14
  122.6 0.7 fusion.17
  123.3 0.7 pad_maximum_fusion.13
  124.0 0.6 broadcast_multiply_fusion.3
  124.6 127.9 %all-reduce.4.cloned.1.call-done = (f32[2,256,128]{2,1,0:T(8,128)}, f32[2,128,128]{2,1,0:T(8,128)}) async-done(((f32[2,256,128]{2,1,0:T(8,128)}, f32[2,128,128]{2,1,0:T(8,128)}), (f32[2,256,128]{2,1,0:T(8,128)}, f32[2,128,128]{2,1,0:T(8,128)})) %all-reduce.4.cloned.1.call-update) | async-done | bytes 393232 | tf_op jit(solution)/shard_map/psum | solution.py:134
  252.5 1.6 broadcast_multiply_fusion.1
  254.1 1.7 broadcast_multiply_fusion
  255.8 2.0 fusion.21
  (37 shorter events, 3.2 us)
Async XLA Ops:
  7.2 245.4 %all-reduce.4.cloned.1.call-start = ((), (), s32[]{:S(2)}) async-start(), calls=%async_computation | async-start | bytes 786432 | tf_op jit(solution)/shard_map/psum | solution.py:134
  7.2 16.4 %collective-permute-start = (bf16[1,64,4096]{2,1,0:T(8,128)(2,1)}, bf16[1,64,4096]{2,1,0:T(8,128)(2,1)S(1)}, u32[]{:S(2)}, u32[]{:S(2)}) collective-permute-start(bf16[1,64,4096]{2,1,0:T(8,128)(2,1)} %param.7), channel_id=1, source_target_pairs={{0,1},{1,2},{2,3},{4,5},{5,6},{6,7},{8,9},{9,10},{10,11},{12,13},{... | collective-permute-start | bytes 1572872 | tf_op jit(solution)/shard_map/ppermute | solution.py:12
  23.6 2.0 copy-start.8
  25.6 0.9 copy-start.10
  26.5 1.0 copy-start.6
  26.5 6.5 %copy-start.5 = (bf16[1,64,4096]{2,1,0:T(8,128)(2,1)S(1)}, bf16[1,64,4096]{2,1,0:T(8,128)(2,1)}, u32[]{:S(2)}) copy-start(bf16[1,64,4096]{2,1,0:T(8,128)(2,1)} %param.13) | copy-start | bytes 1572868
  27.5 15.8 %copy-start.7 = (bf16[2,256,128]{2,1,0:T(8,128)(2,1)S(1)}, bf16[2,256,128]{2,1,0:T(8,128)(2,1)}, u32[]{:S(2)}) copy-start(bf16[2,256,128]{2,1,0:T(8,128)(2,1)} %param.8) | copy-start | bytes 393220
  27.6 15.6 %collective-permute-start.1 = (bf16[1,64,4096]{2,1,0:T(8,128)(2,1)S(1)}, bf16[1,64,4096]{2,1,0:T(8,128)(2,1)S(1)}, u32[]{:S(2)}, u32[]{:S(2)}) collective-permute-start(bf16[1,64,4096]{2,1,0:T(8,128)(2,1)S(1)} %fusion.26), channel_id=1, source_target_pairs={{0,2},{1,3},{4,6},{5,7},{8,10},{9,11},{12,14},{13,15},{16,18},{17,... | collective-permute-start | bytes 1572872 | tf_op jit(solution)/shard_map/ppermute | solution.py:12
  46.0 14.8 %collective-permute-start.2 = (bf16[1,64,4096]{2,1,0:T(8,128)(2,1)S(1)}, bf16[1,64,4096]{2,1,0:T(8,128)(2,1)S(1)}, u32[]{:S(2)}, u32[]{:S(2)}) collective-permute-start(bf16[1,64,4096]{2,1,0:T(8,128)(2,1)S(1)} %slice.203), channel_id=1, source_target_pairs={{2,0},{3,1},{6,4},{7,5},{10,8},{11,9},{14,12},{15,13},{18,16},{19,... | collective-permute-start | bytes 1572872 | tf_op jit(solution)/shard_map/ppermute | solution.py:12
  50.1 10.8 %copy-start.4 = (bf16[1,64,4096]{2,1,0:T(8,128)(2,1)S(1)}, bf16[1,64,4096]{2,1,0:T(8,128)(2,1)}, u32[]{:S(2)}) copy-start(bf16[1,64,4096]{2,1,0:T(8,128)(2,1)} %param.12) | copy-start | bytes 1572868
  62.4 1.1 copy-start
  62.4 1.3 copy-start.2
  117.6 5.0 %copy-start.1 = (bf16[1,128,4096]{2,1,0:T(8,128)(2,1)S(1)}, bf16[1,128,4096]{2,1,0:T(8,128)(2,1)}, u32[]{:S(2)}) copy-start(bf16[1,128,4096]{2,1,0:T(8,128)(2,1)} %copy-done) | copy-start | bytes 3145732
  117.6 5.0 %copy-start.3 = (bf16[1,128,4096]{2,1,0:T(8,128)(2,1)S(1)}, bf16[1,128,4096]{2,1,0:T(8,128)(2,1)}, u32[]{:S(2)}) copy-start(bf16[1,128,4096]{2,1,0:T(8,128)(2,1)} %copy-done.2) | copy-start | bytes 3145732
  117.6 5.0 %copy-start.9 = (bf16[1,64,4096]{2,1,0:T(8,128)(2,1)S(1)}, bf16[1,64,4096]{2,1,0:T(8,128)(2,1)}, u32[]{:S(2)}) copy-start(bf16[1,64,4096]{2,1,0:T(8,128)(2,1)} %copy-done.8) | copy-start | bytes 1572868
  120.6 135.2 %collective-permute-start.3 = (bf16[1,64,4096]{2,1,0:T(8,128)(2,1)}, bf16[1,64,4096]{2,1,0:T(8,128)(2,1)}, u32[]{:S(2)}, u32[]{:S(2)}) collective-permute-start(bf16[1,64,4096]{2,1,0:T(8,128)(2,1)} %slice.202), channel_id=1, source_target_pairs={{1,0},{2,1},{3,2},{5,4},{6,5},{7,6},{9,8},{10,9},{11,10},{13,12},{... | collective-permute-start | bytes 1572872 | tf_op jit(solution)/shard_map/ppermute | solution.py:12
Sparse Core Ops, SparseCore 0:
  124.2 128.3 all-reduce.3
where the time goes:
time: 265 us
  waiting for transfers between devices  157 us (59%)
  blocking collectives  53.3 us (20%)
  between operations  14.3 us (5%)
  starting transfers between devices  12.9 us (5%)
  matrix products  11.3 us (4%)
  other arithmetic  11.3 us (4%)
  local copies, waits for them, and re-layouts  4.41 us (2%)
    psum x1, waiting for transfers between devices, on_device(): lax.psum((jnp.stack([grads_low[0], grads_top[0]]), jnp.stack([grads_low[1...  128 us
    psum x1, blocking collectives, on_device(): lax.psum((jnp.stack([grads_low[0], grads_top[0]]), jnp.stack([grads_low[1...  53.3 us
    ppermute x4, waiting for transfers between devices, from_behind(): return lax.ppermute(block, axis, route)  29.2 us
    ppermute x4, starting transfers between devices, from_behind(): return lax.ppermute(block, axis, route)  12.9 us
  transfers between devices with their start and end apart: 5, of which 4 were waited for; matrix products, arithmetic and copies ran while one was open for 4% of the time, Pallas kernels for 0%

commit v1 on v0

v1 whole, which is shorter than its diff:
```python
import functools
import math

import jax
import jax.numpy as jnp
from jax import lax
from jax.experimental import pallas as pl
from jax.experimental.pallas import tpu as pltpu
from jax.sharding import PartitionSpec as P

MESH = pl.DeviceIdType.MESH
F32 = jnp.float32
BF16 = jnp.bfloat16
CHUNK = 512


def dot(a, b):
    return jnp.dot(a, b, preferred_element_type=F32)


def dot_nt(a, b):
    return lax.dot_general(a, b, (((1,), (1,)), ((), ())), preferred_element_type=F32)


def kernel(
    cfg,
    sig,
    w,
    wb,
    p,
    pb,
    ct,
    cs,
    xtop,
    skip,
    ginp,
    gconv,
    gcbias,
    gout,
    gobias,
    tap0,
    xmid,
    tap1,
    gdel1,
    d1,
    gdel0,
    d0,
    df0,
    dg0,
    z0,
    skip0,
    res1,
    res0,
    wt,
    pt,
    wbc,
    pbc,
    accw,
    accp,
    part,
    rs_buf,
    z_buf,
    total,
    sig_s,
    sig_r,
    x_s,
    x_r,
    d1_s,
    d1_r,
    d0_s,
    d0_r,
    rs_s,
    rs_r,
    z_s,
    z_r,
    ag_s,
    ag_r,
):
    ncor, ntm, nc, t, rows, scale = cfg
    r = sig.shape[1]
    g = p.shape[2]
    g2 = w.shape[1]
    po = p.shape[1]
    me = lax.axis_index("corner")
    zi = lax.axis_index("tm")

    def cols(i):
        return pl.ds(pl.multiple_of(i * t, t), t)

    def shift_copy(src, dst, ssem, rsem, i, distance):
        return pltpu.make_async_remote_copy(
            src_ref=src,
            dst_ref=dst.at[i],
            send_sem=ssem.at[i],
            recv_sem=rsem.at[i],
            device_id={"tm": lax.rem(zi + distance + ntm, ntm)},
            device_id_type=MESH,
        )

    def sig_copy(i):
        return shift_copy(sig.at[0, :, cols(i)], tap0, sig_s, sig_r, i, 1)

    def x_copy(i):
        return shift_copy(xmid.at[i], tap1, x_s, x_r, i, 2)

    def d1_copy(i):
        return shift_copy(gdel1.at[i], d1, d1_s, d1_r, i, -2)

    def d0_copy(i):
        return shift_copy(gdel0.at[i], d0, d0_s, d0_r, i, -1)

    barrier = pltpu.get_barrier_semaphore()

    def greet_corner(j, carry):
        pl.semaphore_signal(
            barrier, inc=1, device_id={"corner": lax.rem(me + j, ncor)}, device_id_type=MESH
        )
        return carry

    def greet_tm(j, carry):
        pl.semaphore_signal(
            barrier, inc=1, device_id={"tm": lax.rem(zi + j, ntm)}, device_id_type=MESH
        )
        return carry

    lax.fori_loop(1, ncor, greet_corner, 0)
    lax.fori_loop(1, ntm, greet_tm, 0)

    for l in range(2):
        wt[l] = w[l].astype(F32).T.astype(BF16)
        pt[l] = p[l].astype(F32).T.astype(BF16)
        wbc[l] = jnp.broadcast_to(wb[l : l + 1, :], (128, g2)).T
        pbc[l] = jnp.broadcast_to(pb[l : l + 1, :], (128, po)).T
    accw[...] = jnp.zeros_like(accw)
    accp[...] = jnp.zeros_like(accp)
    part[...] = jnp.zeros_like(part)

    @pl.when(zi < 1)
    def _():
        tap0[...] = jnp.zeros_like(tap0)

    @pl.when(zi < 2)
    def _():
        tap1[...] = jnp.zeros_like(tap1)

    @pl.when(zi >= ntm - 2)
    def _():
        d1[...] = jnp.zeros_like(d1)

    @pl.when(zi >= ntm - 1)
    def _():
        d0[...] = jnp.zeros_like(d0)

    pl.semaphore_wait(barrier, ncor - 1 + ntm - 1)

    @pl.when(zi < ntm - 1)
    def _():
        def send(i, carry):
            sig_copy(i).start()
            return carry

        lax.fori_loop(0, nc, send, 0)

    ones = jnp.ones((128, t), BF16)

    def wide(ref, l):
        return jnp.concatenate([ref[l]] * (t // 128), axis=1)

    def gates(l, stacked):
        pre = dot(w[l], stacked) + wide(wbc, l)
        th = jnp.tanh(pre[:g])
        sg = 0.5 * jnp.tanh(0.5 * pre[g:]) + 0.5
        z = th * sg
        zb = z.astype(BF16)
        mixed = dot(p[l], zb) + wide(pbc, l)
        return sg - z * th, z - z * sg, zb, mixed

    def accumulate(l, gpre, stacked, u, zb):
        accw[l] += dot_nt(gpre, jnp.concatenate([stacked, ones], axis=0))
        accp[l] += dot_nt(u, jnp.concatenate([zb, ones], axis=0))

    def forward_low(i, carry):
        @pl.when(zi >= 1)
        def _():
            sig_copy(i).wait_recv()

        a = sig[0, :, cols(i)]
        df, dg, zb, mixed = gates(0, jnp.concatenate([tap0[i], a], axis=0))
        xmid[i] = (a.astype(F32) + mixed[:r]).astype(BF16)

        @pl.when(zi < ntm - 2)
        def _():
            x_copy(i).start()

        df0[i] = df
        dg0[i] = dg
        z0[i] = zb
        skip0[i] = mixed[r:]
        return carry

    def top(i, carry):
        @pl.when(zi >= 2)
        def _():
            x_copy(i).wait_recv()

        a = xmid[i]
        stacked = jnp.concatenate([tap1[i], a], axis=0)
        df, dg, zb, mixed = gates(1, stacked)
        c = ct[0, :, cols(i)]
        u = jnp.concatenate([c, cs[0, :, cols(i)]], axis=0)
        gz = dot(pt[1], u)
        gpre = jnp.concatenate([gz * df, gz * dg], axis=0).astype(BF16)
        gin = dot(wt[1], gpre)
        gdel1[i] = gin[:r].astype(BF16)

        @pl.when(zi >= 2)
        def _():
            d1_copy(i).start()

        res1[i] = c.astype(F32) + gin[r:]
        xtop[0, :, cols(i)] = (a.astype(F32) + mixed[:r]).astype(BF16)
        skip[0, :, cols(i)] = (skip0[i] + mixed[r:]).astype(BF16)
        accumulate(1, gpre, stacked, u, zb)
        return carry

    def backward_low(i, carry):
        @pl.when(zi < ntm - 2)
        def _():
            d1_copy(i).wait_recv()

        gm = (res1[i] + d1[i].astype(F32)).astype(BF16)
        u = jnp.concatenate([gm, cs[0, :, cols(i)]], axis=0)
        gz = dot(pt[0], u)
        gpre = jnp.concatenate([gz * df0[i], gz * dg0[i]], axis=0).astype(BF16)
        gin = dot(wt[0], gpre)
        gdel0[i] = gin[:r].astype(BF16)

        @pl.when(zi >= 1)
        def _():
            d0_copy(i).start()

        res0[i] = gm.astype(F32) + gin[r:]
        stacked = jnp.concatenate([tap0[i], sig[0, :, cols(i)]], axis=0)
        accumulate(0, gpre, stacked, u, z0[i])
        return carry

    def finish(i, carry):
        @pl.when(zi < ntm - 1)
        def _():
            d0_copy(i).wait_recv()

        ginp[0, :, cols(i)] = (res0[i] + d0[i].astype(F32)).astype(BF16)
        return carry

    def shard(k):
        return pl.ds(pl.multiple_of(k * rows, 8), rows)

    def rs_copy(l, j):
        to = lax.rem(me + j, ncor)
        return pltpu.make_async_remote_copy(
            src_ref=part.at[l, shard(to)],
            dst_ref=rs_buf.at[l, j - 1],
            send_sem=rs_s.at[l, j - 1],
            recv_sem=rs_r.at[l, j - 1],
            device_id={"corner": to},
            device_id_type=MESH,
        )

    def z_copy(l, j):
        return pltpu.make_async_remote_copy(
            src_ref=z_buf.at[l, zi],
            dst_ref=z_buf.at[l, zi],
            send_sem=z_s.at[l, j - 1],
            recv_sem=z_r.at[l, j - 1],
            device_id={"tm": lax.rem(zi + j, ntm)},
            device_id_type=MESH,
        )

    def z_arrival(l, j):
        origin = lax.rem(zi - j + ntm, ntm)
        return pltpu.make_async_remote_copy(
            src_ref=z_buf.at[l, zi],
            dst_ref=z_buf.at[l, origin],
            send_sem=z_s.at[l, j - 1],
            recv_sem=z_r.at[l, j - 1],
            device_id={"tm": lax.rem(zi + j, ntm)},
            device_id_type=MESH,
        )

    def ag_copy(l, j):
        return pltpu.make_async_remote_copy(
            src_ref=total.at[l, shard(me)],
            dst_ref=total.at[l, shard(me)],
            send_sem=ag_s.at[l, j - 1],
            recv_sem=ag_r.at[l, j - 1],
            device_id={"corner": lax.rem(me + j, ncor)},
            device_id_type=MESH,
        )

    def ag_arrival(l, j):
        return pltpu.make_async_remote_copy(
            src_ref=total.at[l, shard(me)],
            dst_ref=total.at[l, shard(lax.rem(me - j + ncor, ncor))],
            send_sem=ag_s.at[l, j - 1],
            recv_sem=ag_r.at[l, j - 1],
            device_id={"corner": lax.rem(me + j, ncor)},
            device_id_type=MESH,
        )

    def each(n, body):
        def step(j, carry):
            body(j)
            return carry

        lax.fori_loop(1, n, step, 0)

    def rs_start(l):
        part[l, 0:g2] = accw[l, :, 0:128]
        part[l, g2 : g2 + po] = accp[l, :, 0:128]
        brow = accw[l, :, 128:256].T
        for k in range(g2 // 128):
            part[l, g2 + po + k : g2 + po + k + 1] = brow[0:1, k * 128 : (k + 1) * 128]
        prow = accp[l, :, 128:256].T
        at = g2 + po + g2 // 128
        part[l, at : at + 1] = prow[0:1, :]
        each(ncor, lambda j: rs_copy(l, j).start())

    def z_start(l):
        each(ncor, lambda j: rs_copy(l, j).wait_recv())
        s = part[l, shard(me)]
        for j in range(ncor - 1):
            s = s + rs_buf[l, j]
        z_buf[l, zi] = s
        each(ntm, lambda j: z_copy(l, j).start())

    def ag_start(l):
        each(ntm, lambda j: z_arrival(l, j).wait_recv())
        s = z_buf[l, 0]
        for j in range(1, ntm):
            s = s + z_buf[l, j]
        total[l, shard(me)] = s * scale
        each(ncor, lambda j: ag_copy(l, j).start())

    def ag_finish(l):
        each(ncor, lambda j: ag_arrival(l, j).wait_recv())
        gconv[l] = total[l, 0:g2]
        gout[l] = total[l, g2 : g2 + po]
        for k in range(g2 // 128):
            gcbias[l : l + 1, k * 128 : (k + 1) * 128] = total[l, g2 + po + k : g2 + po + k + 1]
        at = g2 + po + g2 // 128
        gobias[l : l + 1, :] = total[l, at : at + 1]

    lax.fori_loop(0, nc, forward_low, 0)
    lax.fori_loop(0, nc, top, 0)
    rs_start(1)
    lax.fori_loop(0, nc // 2, backward_low, 0)
    z_start(1)
    lax.fori_loop(nc // 2, nc, backward_low, 0)
    rs_start(0)
    ag_start(1)
    z_start(0)
    lax.fori_loop(0, nc, finish, 0)
    ag_start(0)
    ag_finish(1)
    ag_finish(0)

    def sent(i, carry):
        @pl.when(zi < ntm - 1)
        def _():
            sig_copy(i).wait_send()

        @pl.when(zi < ntm - 2)
        def _():
            x_copy(i).wait_send()

        @pl.when(zi >= 2)
        def _():
            d1_copy(i).wait_send()

        @pl.when(zi >= 1)
        def _():
            d0_copy(i).wait_send()

        return carry

    lax.fori_loop(0, nc, sent, 0)
    for l in range(2):
        each(ncor, lambda j: rs_copy(l, j).wait_send())
        each(ntm, lambda j: z_copy(l, j).wait_send())
        each(ncor, lambda j: ag_copy(l, j).wait_send())


def on_device(sig, w, wb, p, pb, ct, cs):
    ncor = lax.axis_size("corner")
    ntm = lax.axis_size("tm")
    _, r, time = sig.shape
    _, g2, _ = w.shape
    _, po, g = p.shape
    t = CHUNK
    nc = time // t
    used = g2 + po + g2 // 128 + 1
    rows = -(-used // (ncor * 8)) * 8
    count = sig.shape[0] * ncor * time * ntm
    cfg = (ncor, ntm, nc, t, rows, 1.0 / math.sqrt(count))
    vmem = pl.BlockSpec(memory_space=pltpu.VMEM)
    dma = pltpu.SemaphoreType.DMA
    field = pltpu.VMEM((nc, r, t), BF16)
    field32 = pltpu.VMEM((nc, r, t), F32)
    flops = 2 * 2 * time * 3 * (g2 * 2 * r + po * g)
    return pl.pallas_call(
        functools.partial(kernel, cfg),
        out_shape=(
            jax.ShapeDtypeStruct(sig.shape, BF16),
            jax.ShapeDtypeStruct(sig.shape, BF16),
            jax.ShapeDtypeStruct(sig.shape, BF16),
            jax.ShapeDtypeStruct(w.shape, F32),
            jax.ShapeDtypeStruct(wb.shape, F32),
            jax.ShapeDtypeStruct(p.shape, F32),
            jax.ShapeDtypeStruct(pb.shape, F32),
        ),
        in_specs=[vmem] * 7,
        out_specs=[vmem] * 7,
        scratch_shapes=[
            field,
            field,
            field,
            field,
            field,
            field,
            field,
            pltpu.VMEM((nc, g, t), F32),
            pltpu.VMEM((nc, g, t), F32),
            pltpu.VMEM((nc, g, t), BF16),
            field32,
            field32,
            field32,
            pltpu.VMEM((2, w.shape[2], g2), BF16),
            pltpu.VMEM((2, g, po), BF16),
            pltpu.VMEM((2, g2, 128), F32),
            pltpu.VMEM((2, po, 128), F32),
            pltpu.VMEM((2, g2, 256), F32),
            pltpu.VMEM((2, po, 256), F32),
            pltpu.VMEM((2, ncor * rows, 128), F32),
            pltpu.VMEM((2, ncor - 1, rows, 128), F32),
            pltpu.VMEM((2, ntm, rows, 128), F32),
            pltpu.VMEM((2, ncor * rows, 128), F32),
        ]
        + [dma((nc,))] * 8
        + [dma((2, ncor - 1))] * 2
        + [dma((2, ntm - 1))] * 2
        + [dma((2, ncor - 1))] * 2,
        compiler_params=pltpu.CompilerParams(
            collective_id=0, has_side_effects=True, vmem_limit_bytes=48 * 1024 * 1024
        ),
        cost_estimate=pl.CostEstimate(
            flops=flops, bytes_accessed=6 * sig.size * 2, transcendentals=2 * g2 * time
        ),
    )(sig, w, wb, p, pb, ct, cs)


def solution(mesh):
    field = P("corner", None, "tm")
    return jax.shard_map(
        on_device,
        mesh=mesh,
        in_specs=(field, P(), P(), P(), P(), field, field),
        out_specs=(field, field, field, P(), P(), P(), P()),
        check_vma=False,
    )
```

time: 265 us -> 81.9 us (0.31)
  waiting for transfers between devices: 157 us -> 0 us
  Pallas kernels: 0 us -> 69.8 us
  blocking collectives: 53.3 us -> 0 us
  between operations: 14.3 us -> 0.66 us
  starting transfers between devices: 12.9 us -> 0 us
  matrix products: 11.3 us -> 0 us
  other arithmetic: 11.3 us -> 0 us
  local copies, waits for them, and re-layouts: 4.41 us -> 11.1 us
    psum x1 -> x0, waiting for transfers between devices: 128 us -> none  [on_device(): lax.psum((jnp.stack([grads_low[0], grads_top[0]]), jnp.stack([grads_low[1...]
    pallas_call x0 -> x1, Pallas kernels: none -> 69.8 us  [on_device(): pl.pallas_call(functools.partial(kernel, cfg), out_shape=(jax.ShapeDtypeS...]
    psum x1 -> x0, blocking collectives: 53.3 us -> none  [on_device(): lax.psum((jnp.stack([grads_low[0], grads_top[0]]), jnp.stack([grads_low[1...]
    ppermute x4 -> x0, waiting for transfers between devices: 29.2 us -> none  [from_behind(): return lax.ppermute(block, axis, route)]
    ppermute x4 -> x0, starting transfers between devices: 12.9 us -> none  [from_behind(): return lax.ppermute(block, axis, route)]
    dot_general x12 -> x0, matrix products: 11.3 us -> none  [the longest x2 2.84 us: layer_backward(): jnp.einsum('og,bot->bgt', proj, upper, preferred_element_type=jnp.float32)]
    unnamed x23 -> x21, local copies, waits for them, and re-layouts: 1.95 us -> 11.1 us
    mul x4 -> x0, other arithmetic: 4.39 us -> none  [the longest x1 1.67 us: on_device(): summed[0] * scale]
  transfers between devices with their start and end apart: 5 -> 0, of which waited for: 4 -> 0; matrix products, arithmetic and copies ran while one was open for 4% -> 0% of each run, Pallas kernels for 0% -> 0%
where the time goes in v1:
time: 81.9 us; the launch traced here: 81.6 us
  Pallas kernels  69.8 us (85%)
  local copies, waits for them, and re-layouts  11.1 us (14%)
    pallas_call x1, Pallas kernels, on_device(): pl.pallas_call(functools.partial(kernel, cfg), out_shape=(jax.ShapeDtypeS...  69.8 us
    unnamed x21, local copies, waits for them, and re-layouts  11.1 us

profile of v1, /device:TPU:0, one launch (start us, length us, event | category | flops | bytes accessed | tf_op | source)
XLA Modules:
  0.0 81.6 jit_solution(6688902359033100431)
XLA Ops:
  0.6 0.0 copy-start
  0.6 1.0 %copy-done = bf16[1,64,4096]{2,1,0:T(8,128)(2,1)S(1)} copy-done((bf16[1,64,4096]{2,1,0:T(8,128)(2,1)S(1)}, bf16[1,64,4096]{2,1,0:T(8,128)(2,1)}, u32[]{:S(2)}) %copy-start) | copy-done | bytes 524312
  1.7 0.0 copy-start.1
  1.7 1.0 %copy-done.1 = bf16[1,64,4096]{2,1,0:T(8,128)(2,1)S(1)} copy-done((bf16[1,64,4096]{2,1,0:T(8,128)(2,1)S(1)}, bf16[1,64,4096]{2,1,0:T(8,128)(2,1)}, u32[]{:S(2)}) %copy-start.1) | copy-done | bytes 524312
  2.7 0.0 copy-start.2
  2.7 1.0 %copy-done.2 = bf16[1,64,4096]{2,1,0:T(8,128)(2,1)S(1)} copy-done((bf16[1,64,4096]{2,1,0:T(8,128)(2,1)S(1)}, bf16[1,64,4096]{2,1,0:T(8,128)(2,1)}, u32[]{:S(2)}) %copy-start.2) | copy-done | bytes 524312
  3.8 0.0 copy-start.3
  3.8 0.9 %copy-done.3 = bf16[2,256,128]{2,1,0:T(8,128)(2,1)S(1)} copy-done((bf16[2,256,128]{2,1,0:T(8,128)(2,1)S(1)}, bf16[2,256,128]{2,1,0:T(8,128)(2,1)}, u32[]{:S(2)}) %copy-start.3) | copy-done | bytes 131096
  4.7 0.0 copy-start.4
  4.7 0.8 %copy-done.4 = bf16[2,128,128]{2,1,0:T(8,128)(2,1)S(1)} copy-done((bf16[2,128,128]{2,1,0:T(8,128)(2,1)S(1)}, bf16[2,128,128]{2,1,0:T(8,128)(2,1)}, u32[]{:S(2)}) %copy-start.4) | copy-done | bytes 65560
  5.5 0.0 copy-start.5
  5.5 0.7 copy-done.5
  6.2 0.0 copy-start.6
  6.2 0.7 copy-done.6
  6.9 69.8 %shard_map.126 = (bf16[1,64,4096]{2,1,0:T(8,128)(2,1)S(1)}, bf16[1,64,4096]{2,1,0:T(8,128)(2,1)S(1)}, bf16[1,64,4096]{2,1,0:T(8,128)(2,1)S(1)}, f32[2,256,128]{2...) custom-call(bf16[1,64,4096]{2,1,0:T(8,128)(2,1)S(1)} %copy-done, ...), custom_call_target="tpu_custom_call" | custom-call | flops 2415919104 | bytes 3145728 | tf_op jit(solution)/shard_map/pallas_call | solution.py:410
  76.7 0.8 copy.21
  77.5 0.8 copy.22
  78.3 0.8 copy.23
  79.1 0.7 copy.24
  79.8 0.6 copy.25
  80.4 0.7 copy.26
  81.0 0.6 copy.27
Async XLA Ops:
  0.6 1.0 %copy-start = (bf16[1,64,4096]{2,1,0:T(8,128)(2,1)S(1)}, bf16[1,64,4096]{2,1,0:T(8,128)(2,1)}, u32[]{:S(2)}) copy-start(bf16[1,64,4096]{2,1,0:T(8,128)(2,1)} %sig.1) | copy-start | bytes 1572868
  1.7 1.0 %copy-start.1 = (bf16[1,64,4096]{2,1,0:T(8,128)(2,1)S(1)}, bf16[1,64,4096]{2,1,0:T(8,128)(2,1)}, u32[]{:S(2)}) copy-start(bf16[1,64,4096]{2,1,0:T(8,128)(2,1)} %ct.1) | copy-start | bytes 1572868
  2.7 1.0 %copy-start.2 = (bf16[1,64,4096]{2,1,0:T(8,128)(2,1)S(1)}, bf16[1,64,4096]{2,1,0:T(8,128)(2,1)}, u32[]{:S(2)}) copy-start(bf16[1,64,4096]{2,1,0:T(8,128)(2,1)} %cs.1) | copy-start | bytes 1572868
  3.8 0.9 %copy-start.3 = (bf16[2,256,128]{2,1,0:T(8,128)(2,1)S(1)}, bf16[2,256,128]{2,1,0:T(8,128)(2,1)}, u32[]{:S(2)}) copy-start(bf16[2,256,128]{2,1,0:T(8,128)(2,1)} %w.1) | copy-start | bytes 393220
  4.7 0.8 %copy-start.4 = (bf16[2,128,128]{2,1,0:T(8,128)(2,1)S(1)}, bf16[2,128,128]{2,1,0:T(8,128)(2,1)}, u32[]{:S(2)}) copy-start(bf16[2,128,128]{2,1,0:T(8,128)(2,1)} %p.1) | copy-start | bytes 196612
  5.5 0.7 copy-start.5
  6.2 0.7 copy-start.6

commit v2 on v1

--- a/solution.py
+++ b/solution.py
@@ -12,6 +12,7 @@
 F32 = jnp.float32
 BF16 = jnp.bfloat16
 CHUNK = 512
+LAG = 2
 
 
 def dot(a, b):
@@ -24,6 +25,20 @@
 
 def kernel(
     cfg,
+    sig_h,
+    w_h,
+    wb_h,
+    p_h,
+    pb_h,
+    ct_h,
+    cs_h,
+    xtop_h,
+    skip_h,
+    ginp_h,
+    gconv_h,
+    gcbias_h,
+    gout_h,
+    gobias_h,
     sig,
     w,
     wb,
@@ -31,13 +46,13 @@
     pb,
     ct,
     cs,
+    in_s,
     xtop,
     skip,
     ginp,
-    gconv,
     gcbias,
-    gout,
     gobias,
+    out_s,
     tap0,
     xmid,
     tap1,
@@ -77,6 +92,7 @@
     ag_r,
 ):
     ncor, ntm, nc, t, rows, scale = cfg
+    lag = min(LAG, nc)
     r = sig.shape[1]
     g = p.shape[2]
     g2 = w.shape[1]
@@ -109,6 +125,15 @@
     def d0_copy(i):
         return shift_copy(gdel0.at[i], d0, d0_s, d0_r, i, -1)
 
+    moves = [
+        pltpu.make_async_copy(a, b, in_s.at[k])
+        for k, (a, b) in enumerate(
+            ((sig_h, sig), (w_h, w), (wb_h, wb), (p_h, p), (pb_h, pb), (ct_h, ct), (cs_h, cs))
+        )
+    ]
+    for m in moves:
+        m.start()
+
     barrier = pltpu.get_barrier_semaphore()
 
     def greet_corner(j, carry):
@@ -126,6 +151,8 @@
     lax.fori_loop(1, ncor, greet_corner, 0)
     lax.fori_loop(1, ntm, greet_tm, 0)
 
+    for m in moves:
+        m.wait()
     for l in range(2):
         wt[l] = w[l].astype(F32).T.astype(BF16)
         pt[l] = p[l].astype(F32).T.astype(BF16)
@@ -187,22 +214,38 @@
         a = sig[0, :, cols(i)]
         df, dg, zb, mixed = gates(0, jnp.concatenate([tap0[i], a], axis=0))
         xmid[i] = (a.astype(F32) + mixed[:r]).astype(BF16)
-
-        @pl.when(zi < ntm - 2)
-        def _():
-            x_copy(i).start()
-
         df0[i] = df
         dg0[i] = dg
         z0[i] = zb
         skip0[i] = mixed[r:]
-        return carry
-
-    def top(i, carry):
+
+        @pl.when(zi < ntm - 2)
+        def _():
+            x_copy(i).start()
+
+        return carry
+
+    def wait_x(i):
         @pl.when(zi >= 2)
         def _():
             x_copy(i).wait_recv()
 
+    def send_d1(i):
+        @pl.when(zi >= 2)
+        def _():
+            d1_copy(i).start()
+
+    def wait_d1(i):
+        @pl.when(zi < ntm - 2)
+        def _():
+            d1_copy(i).wait_recv()
+
+    def send_d0(i):
+        @pl.when(zi >= 1)
+        def _():
+            d0_copy(i).start()
+
+    def top(i):
         a = xmid[i]
         stacked = jnp.concatenate([tap1[i], a], axis=0)
         df, dg, zb, mixed = gates(1, stacked)
@@ -212,36 +255,41 @@
         gpre = jnp.concatenate([gz * df, gz * dg], axis=0).astype(BF16)
         gin = dot(wt[1], gpre)
         gdel1[i] = gin[:r].astype(BF16)
-
-        @pl.when(zi >= 2)
-        def _():
-            d1_copy(i).start()
-
         res1[i] = c.astype(F32) + gin[r:]
         xtop[0, :, cols(i)] = (a.astype(F32) + mixed[:r]).astype(BF16)
         skip[0, :, cols(i)] = (skip0[i] + mixed[r:]).astype(BF16)
         accumulate(1, gpre, stacked, u, zb)
-        return carry
-
-    def backward_low(i, carry):
-        @pl.when(zi < ntm - 2)
-        def _():
-            d1_copy(i).wait_recv()
-
+
+    def low(i):
         gm = (res1[i] + d1[i].astype(F32)).astype(BF16)
         u = jnp.concatenate([gm, cs[0, :, cols(i)]], axis=0)
         gz = dot(pt[0], u)
         gpre = jnp.concatenate([gz * df0[i], gz * dg0[i]], axis=0).astype(BF16)
         gin = dot(wt[0], gpre)
         gdel0[i] = gin[:r].astype(BF16)
-
-        @pl.when(zi >= 1)
-        def _():
-            d0_copy(i).start()
-
         res0[i] = gm.astype(F32) + gin[r:]
         stacked = jnp.concatenate([tap0[i], sig[0, :, cols(i)]], axis=0)
         accumulate(0, gpre, stacked, u, z0[i])
+
+    def top_only(i, carry):
+        wait_x(i)
+        top(i)
+        send_d1(i)
+        return carry
+
+    def both(i, carry):
+        wait_x(i)
+        wait_d1(i - lag)
+        low(i - lag)
+        top(i)
+        send_d1(i)
+        send_d0(i - lag)
+        return carry
+
+    def low_only(i, carry):
+        wait_d1(i)
+        low(i)
+        send_d0(i)
         return carry
 
     def finish(i, carry):
@@ -306,6 +354,9 @@
             device_id={"corner": lax.rem(me + j, ncor)},
             device_id_type=MESH,
         )
+
+    def put(src, dst, k):
+        return pltpu.make_async_copy(src, dst, out_s.at[k])
 
     def each(n, body):
         def step(j, carry):
@@ -343,26 +394,40 @@
 
     def ag_finish(l):
         each(ncor, lambda j: ag_arrival(l, j).wait_recv())
-        gconv[l] = total[l, 0:g2]
-        gout[l] = total[l, g2 : g2 + po]
+        put(total.at[l, 0:g2], gconv_h.at[l], 5 + l).start()
+        put(total.at[l, g2 : g2 + po], gout_h.at[l], 7 + l).start()
         for k in range(g2 // 128):
             gcbias[l : l + 1, k * 128 : (k + 1) * 128] = total[l, g2 + po + k : g2 + po + k + 1]
         at = g2 + po + g2 // 128
         gobias[l : l + 1, :] = total[l, at : at + 1]
 
     lax.fori_loop(0, nc, forward_low, 0)
-    lax.fori_loop(0, nc, top, 0)
+    lax.fori_loop(0, lag, top_only, 0)
+    lax.fori_loop(lag, nc, both, 0)
     rs_start(1)
-    lax.fori_loop(0, nc // 2, backward_low, 0)
+    put(xtop, xtop_h, 0).start()
+    put(skip, skip_h, 1).start()
+    lax.fori_loop(nc - lag, nc, low_only, 0)
+    rs_start(0)
     z_start(1)
-    lax.fori_loop(nc // 2, nc, backward_low, 0)
-    rs_start(0)
+    z_start(0)
     ag_start(1)
-    z_start(0)
     lax.fori_loop(0, nc, finish, 0)
+    put(ginp, ginp_h, 2).start()
     ag_start(0)
     ag_finish(1)
     ag_finish(0)
+    put(gcbias, gcbias_h, 3).start()
+    put(gobias, gobias_h, 4).start()
+
+    put(xtop, xtop_h, 0).wait()
+    put(skip, skip_h, 1).wait()
+    put(ginp, ginp_h, 2).wait()
+    put(gcbias, gcbias_h, 3).wait()
+    put(gobias, gobias_h, 4).wait()
+    for l in range(2):
+        put(total.at[l, 0:g2], gconv_h.at[l], 5 + l).wait()
+        put(total.at[l, g2 : g2 + po], gout_h.at[l], 7 + l).wait()
 
     def sent(i, carry):
         @pl.when(zi < ntm - 1)
@@ -388,6 +453,15 @@
         each(ncor, lambda j: rs_copy(l, j).wait_send())
         each(ntm, lambda j: z_copy(l, j).wait_send())
         each(ncor, lambda j: ag_copy(l, j).wait_send())
+
+
+def deliver(*refs):
+    sems = refs[14]
+    moves = [pltpu.make_async_copy(refs[k], refs[7 + k], sems.at[k]) for k in range(7)]
+    for m in moves:
+        m.start()
+    for m in moves:
+        m.wait()
 
 
 def on_device(sig, w, wb, p, pb, ct, cs):
@@ -402,12 +476,14 @@
     rows = -(-used // (ncor * 8)) * 8
     count = sig.shape[0] * ncor * time * ntm
     cfg = (ncor, ntm, nc, t, rows, 1.0 / math.sqrt(count))
-    vmem = pl.BlockSpec(memory_space=pltpu.VMEM)
+    hbm = pl.BlockSpec(memory_space=pltpu.HBM)
+    room = 62 * 1024 * 1024
     dma = pltpu.SemaphoreType.DMA
     field = pltpu.VMEM((nc, r, t), BF16)
     field32 = pltpu.VMEM((nc, r, t), F32)
     flops = 2 * 2 * time * 3 * (g2 * 2 * r + po * g)
-    return pl.pallas_call(
+    args = (sig, w, wb, p, pb, ct, cs)
+    outs = pl.pallas_call(
         functools.partial(kernel, cfg),
         out_shape=(
             jax.ShapeDtypeStruct(sig.shape, BF16),
@@ -418,9 +494,17 @@
             jax.ShapeDtypeStruct(p.shape, F32),
             jax.ShapeDtypeStruct(pb.shape, F32),
         ),
-        in_specs=[vmem] * 7,
-        out_specs=[vmem] * 7,
-        scratch_shapes=[
+        in_specs=[hbm] * 7,
+        out_specs=[hbm] * 7,
+        scratch_shapes=[pltpu.VMEM(a.shape, a.dtype) for a in args]
+        + [
+            dma((7,)),
+            pltpu.VMEM(sig.shape, BF16),
+            pltpu.VMEM(sig.shape, BF16),
+            pltpu.VMEM(sig.shape, BF16),
+            pltpu.VMEM(wb.shape, F32),
+            pltpu.VMEM(pb.shape, F32),
+            dma((9,)),
             field,
             field,
             field,
@@ -450,12 +534,20 @@
         + [dma((2, ntm - 1))] * 2
         + [dma((2, ncor - 1))] * 2,
         compiler_params=pltpu.CompilerParams(
-            collective_id=0, has_side_effects=True, vmem_limit_bytes=48 * 1024 * 1024
+            collective_id=0, has_side_effects=True, vmem_limit_bytes=room
         ),
         cost_estimate=pl.CostEstimate(
             flops=flops, bytes_accessed=6 * sig.size * 2, transcendentals=2 * g2 * time
         ),
-    )(sig, w, wb, p, pb, ct, cs)
+    )(*args)
+    return pl.pallas_call(
+        deliver,
+        out_shape=tuple(jax.ShapeDtypeStruct(a.shape, a.dtype) for a in outs),
+        in_specs=[hbm] * 7,
+        out_specs=[hbm] * 7,
+        scratch_shapes=[dma((7,))],
+        compiler_params=pltpu.CompilerParams(vmem_limit_bytes=room),
+    )(*outs)
 
 
 def solution(mesh):

time: 81.9 us -> 132 us (1.61)
  Pallas kernels: 69.8 us -> 131 us
  local copies, waits for them, and re-layouts: 11.1 us -> 0 us
    pallas_call x0 -> x1, Pallas kernels: none -> 60.8 us  [on_device(): pl.pallas_call(deliver, out_shape=tuple((jax.ShapeDtypeStruct(a.shape, a....]
    unnamed x21 -> x0, local copies, waits for them, and re-layouts: 11.1 us -> none
where the time goes in v2:
time: 132 us
  Pallas kernels  131 us (99%)
    pallas_call x1, Pallas kernels, on_device(): pl.pallas_call(functools.partial(kernel, cfg), out_shape=(jax.ShapeDtypeS...  70.6 us
    pallas_call x1, Pallas kernels, on_device(): pl.pallas_call(deliver, out_shape=tuple((jax.ShapeDtypeStruct(a.shape, a....  60.8 us

profile of v2, /device:TPU:0, one launch (start us, length us, event | category | flops | bytes accessed | tf_op | source)
XLA Modules:
  0.0 132.1 jit_solution(14890453814004412844)
XLA Ops:
  0.6 70.6 %shard_map.126 = (bf16[1,64,4096]{2,1,0:T(8,128)(2,1)}, bf16[1,64,4096]{2,1,0:T(8,128)(2,1)}, bf16[1,64,4096]{2,1,0:T(8,128)(2,1)}, f32[2,256,128]{2,1,0:T(8,128...) custom-call(bf16[1,64,4096]{2,1,0:T(8,128)(2,1)} %sig_h.1, bf16[2,256,128]{2,1,0:T(8,128)(2,1)} %w_h.1, ...), custom_call_target="tpu_custom_call" | custom-call | flops 2415919104 | bytes 3145728 | tf_op jit(solution)/shard_map/pallas_call | solution.py:486
  71.2 60.8 %shard_map.127 = (bf16[1,64,4096]{2,1,0:T(8,128)(2,1)}, bf16[1,64,4096]{2,1,0:T(8,128)(2,1)}, bf16[1,64,4096]{2,1,0:T(8,128)(2,1)}, f32[2,256,128]{2,1,0:T(8,128...) custom-call(bf16[1,64,4096]{2,1,0:T(8,128)(2,1)} %get-tuple-element.14.refs_0_, ...), custom_call_target="tpu_custom_call" | custom-call | tf_op jit(solution)/shard_map/pallas_call | solution.py:543

commit v3 on v2

--- a/solution.py
+++ b/solution.py
@@ -50,7 +50,9 @@
     xtop,
     skip,
     ginp,
+    gconv,
     gcbias,
+    gout,
     gobias,
     out_s,
     tap0,
@@ -72,6 +74,7 @@
     pbc,
     accw,
     accp,
+    bias,
     part,
     rs_buf,
     z_buf,
@@ -161,6 +164,7 @@
     accw[...] = jnp.zeros_like(accw)
     accp[...] = jnp.zeros_like(accp)
     part[...] = jnp.zeros_like(part)
+    bias[...] = jnp.zeros_like(bias)
 
     @pl.when(zi < 1)
     def _():
@@ -301,59 +305,37 @@
         return carry
 
     def shard(k):
-        return pl.ds(pl.multiple_of(k * rows, 8), rows)
-
-    def rs_copy(l, j):
+        return pl.ds(pl.multiple_of(k * rows, 16), rows)
+
+    def reduce_copy(src, dst, ssem, rsem, j, axis, to):
+        return pltpu.make_async_remote_copy(
+            src_ref=src,
+            dst_ref=dst,
+            send_sem=ssem.at[j - 1],
+            recv_sem=rsem.at[j - 1],
+            device_id={axis: to},
+            device_id_type=MESH,
+        )
+
+    def rs_copy(j):
         to = lax.rem(me + j, ncor)
-        return pltpu.make_async_remote_copy(
-            src_ref=part.at[l, shard(to)],
-            dst_ref=rs_buf.at[l, j - 1],
-            send_sem=rs_s.at[l, j - 1],
-            recv_sem=rs_r.at[l, j - 1],
-            device_id={"corner": to},
-            device_id_type=MESH,
-        )
-
-    def z_copy(l, j):
-        return pltpu.make_async_remote_copy(
-            src_ref=z_buf.at[l, zi],
-            dst_ref=z_buf.at[l, zi],
-            send_sem=z_s.at[l, j - 1],
-            recv_sem=z_r.at[l, j - 1],
-            device_id={"tm": lax.rem(zi + j, ntm)},
-            device_id_type=MESH,
-        )
-
-    def z_arrival(l, j):
-        origin = lax.rem(zi - j + ntm, ntm)
-        return pltpu.make_async_remote_copy(
-            src_ref=z_buf.at[l, zi],
-            dst_ref=z_buf.at[l, origin],
-            send_sem=z_s.at[l, j - 1],
-            recv_sem=z_r.at[l, j - 1],
-            device_id={"tm": lax.rem(zi + j, ntm)},
-            device_id_type=MESH,
-        )
-
-    def ag_copy(l, j):
-        return pltpu.make_async_remote_copy(
-            src_ref=total.at[l, shard(me)],
-            dst_ref=total.at[l, shard(me)],
-            send_sem=ag_s.at[l, j - 1],
-            recv_sem=ag_r.at[l, j - 1],
-            device_id={"corner": lax.rem(me + j, ncor)},
-            device_id_type=MESH,
-        )
-
-    def ag_arrival(l, j):
-        return pltpu.make_async_remote_copy(
-            src_ref=total.at[l, shard(me)],
-            dst_ref=total.at[l, shard(lax.rem(me - j + ncor, ncor))],
-            send_sem=ag_s.at[l, j - 1],
-            recv_sem=ag_r.at[l, j - 1],
-            device_id={"corner": lax.rem(me + j, ncor)},
-            device_id_type=MESH,
-        )
+        return reduce_copy(part.at[shard(to)], rs_buf.at[j - 1], rs_s, rs_r, j, "corner", to)
+
+    def z_copy(j, slot):
+        to = lax.rem(zi + j, ntm)
+        return reduce_copy(z_buf.at[zi], z_buf.at[slot], z_s, z_r, j, "tm", to)
+
+    def ag_copy(j, owner):
+        to = lax.rem(me + j, ncor)
+        return reduce_copy(
+            total.at[shard(me)], total.at[shard(owner)], ag_s, ag_r, j, "corner", to
+        )
+
+    def z_from(j):
+        return lax.rem(zi - j + ntm, ntm)
+
+    def ag_from(j):
+        return lax.rem(me - j + ncor, ncor)
 
     def put(src, dst, k):
         return pltpu.make_async_copy(src, dst, out_s.at[k])
@@ -365,69 +347,69 @@
 
         lax.fori_loop(1, n, step, 0)
 
-    def rs_start(l):
-        part[l, 0:g2] = accw[l, :, 0:128]
-        part[l, g2 : g2 + po] = accp[l, :, 0:128]
+    mats = g2 + po
+    cuts = g2 // 128
+
+    def fill(l):
+        part[l * mats : l * mats + g2] = accw[l, :, 0:128].astype(BF16)
+        part[l * mats + g2 : (l + 1) * mats] = accp[l, :, 0:128].astype(BF16)
         brow = accw[l, :, 128:256].T
-        for k in range(g2 // 128):
-            part[l, g2 + po + k : g2 + po + k + 1] = brow[0:1, k * 128 : (k + 1) * 128]
-        prow = accp[l, :, 128:256].T
-        at = g2 + po + g2 // 128
-        part[l, at : at + 1] = prow[0:1, :]
-        each(ncor, lambda j: rs_copy(l, j).start())
-
-    def z_start(l):
-        each(ncor, lambda j: rs_copy(l, j).wait_recv())
-        s = part[l, shard(me)]
+        for k in range(cuts):
+            at = l * (cuts + 1) + k
+            bias[at : at + 1] = brow[0:1, k * 128 : (k + 1) * 128]
+        at = l * (cuts + 1) + cuts
+        bias[at : at + 1] = accp[l, :, 128:256].T[0:1, :]
+
+    def rs_start():
+        part[2 * mats : 2 * mats + 16] = bias[...].astype(BF16)
+        each(ncor, lambda j: rs_copy(j).start())
+
+    def z_start():
+        each(ncor, lambda j: rs_copy(j).wait_recv())
+        s = part[shard(me)].astype(F32)
         for j in range(ncor - 1):
-            s = s + rs_buf[l, j]
-        z_buf[l, zi] = s
-        each(ntm, lambda j: z_copy(l, j).start())
-
-    def ag_start(l):
-        each(ntm, lambda j: z_arrival(l, j).wait_recv())
-        s = z_buf[l, 0]
+            s = s + rs_buf[j].astype(F32)
+        z_buf[zi] = s.astype(BF16)
+        each(ntm, lambda j: z_copy(j, zi).start())
+
+    def ag_start():
+        each(ntm, lambda j: z_copy(j, z_from(j)).wait_recv())
+        s = z_buf[0].astype(F32)
         for j in range(1, ntm):
-            s = s + z_buf[l, j]
-        total[l, shard(me)] = s * scale
-        each(ncor, lambda j: ag_copy(l, j).start())
-
-    def ag_finish(l):
-        each(ncor, lambda j: ag_arrival(l, j).wait_recv())
-        put(total.at[l, 0:g2], gconv_h.at[l], 5 + l).start()
-        put(total.at[l, g2 : g2 + po], gout_h.at[l], 7 + l).start()
-        for k in range(g2 // 128):
-            gcbias[l : l + 1, k * 128 : (k + 1) * 128] = total[l, g2 + po + k : g2 + po + k + 1]
-        at = g2 + po + g2 // 128
-        gobias[l : l + 1, :] = total[l, at : at + 1]
+            s = s + z_buf[j].astype(F32)
+        total[shard(me)] = (s * scale).astype(BF16)
+        each(ncor, lambda j: ag_copy(j, me).start())
+
+    def ag_finish():
+        each(ncor, lambda j: ag_copy(j, ag_from(j)).wait_recv())
+        tail = total[2 * mats : 2 * mats + 16].astype(F32)
+        for l in range(2):
+            gconv[l] = total[l * mats : l * mats + g2].astype(F32)
+            gout[l] = total[l * mats + g2 : (l + 1) * mats].astype(F32)
+            for k in range(cuts):
+                at = l * (cuts + 1) + k
+                gcbias[l : l + 1, k * 128 : (k + 1) * 128] = tail[at : at + 1]
+            at = l * (cuts + 1) + cuts
+            gobias[l : l + 1, :] = tail[at : at + 1]
 
     lax.fori_loop(0, nc, forward_low, 0)
     lax.fori_loop(0, lag, top_only, 0)
     lax.fori_loop(lag, nc, both, 0)
-    rs_start(1)
     put(xtop, xtop_h, 0).start()
     put(skip, skip_h, 1).start()
+    fill(1)
     lax.fori_loop(nc - lag, nc, low_only, 0)
-    rs_start(0)
-    z_start(1)
-    z_start(0)
-    ag_start(1)
+    fill(0)
+    rs_start()
+    z_start()
     lax.fori_loop(0, nc, finish, 0)
     put(ginp, ginp_h, 2).start()
-    ag_start(0)
-    ag_finish(1)
-    ag_finish(0)
-    put(gcbias, gcbias_h, 3).start()
-    put(gobias, gobias_h, 4).start()
-
-    put(xtop, xtop_h, 0).wait()
-    put(skip, skip_h, 1).wait()
-    put(ginp, ginp_h, 2).wait()
-    put(gcbias, gcbias_h, 3).wait()
-    put(gobias, gobias_h, 4).wait()
-    for l in range(2):
-        put(total.at[l, 0:g2], gconv_h.at[l], 5 + l).wait()
-        put(total.at[l, g2 : g2 + po], gout_h.at[l], 7 + l).wait()
+    ag_start()
+    ag_finish()
+    for k, (a, b) in enumerate(
+        ((gconv, gconv_h), (gcbias, gcbias_h), (gout, gout_h), (gobias, gobias_h))
+    ):
+        put(a, b, 3 + k).start()
 
     def sent(i, carry):
         @pl.when(zi < ntm - 1)
@@ -449,19 +431,34 @@
         return carry
 
     lax.fori_loop(0, nc, sent, 0)
-    for l in range(2):
-        each(ncor, lambda j: rs_copy(l, j).wait_send())
-        each(ntm, lambda j: z_copy(l, j).wait_send())
-        each(ncor, lambda j: ag_copy(l, j).wait_send())
+    each(ncor, lambda j: rs_copy(j).wait_send())
+    each(ntm, lambda j: z_copy(j, zi).wait_send())
+    each(ncor, lambda j: ag_copy(j, me).wait_send())
+    for k, (a, b) in enumerate(
+        (
+            (xtop, xtop_h),
+            (skip, skip_h),
+            (ginp, ginp_h),
+            (gconv, gconv_h),
+            (gcbias, gcbias_h),
+            (gout, gout_h),
+            (gobias, gobias_h),
+        )
+    ):
+        put(a, b, k).wait()
 
 
 def deliver(*refs):
-    sems = refs[14]
-    moves = [pltpu.make_async_copy(refs[k], refs[7 + k], sems.at[k]) for k in range(7)]
-    for m in moves:
+    held, sems = refs[14:21], refs[21]
+    ins = [pltpu.make_async_copy(refs[k], held[k], sems.at[0, k]) for k in range(7)]
+    outs = [pltpu.make_async_copy(held[k], refs[7 + k], sems.at[1, k]) for k in range(7)]
+    for m in ins:
         m.start()
-    for m in moves:
-        m.wait()
+    for a, b in zip(ins, outs):
+        a.wait()
+        b.start()
+    for b in outs:
+        b.wait()
 
 
 def on_device(sig, w, wb, p, pb, ct, cs):
@@ -472,8 +469,8 @@
     _, po, g = p.shape
     t = CHUNK
     nc = time // t
-    used = g2 + po + g2 // 128 + 1
-    rows = -(-used // (ncor * 8)) * 8
+    used = 2 * (g2 + po) + 16
+    rows = -(-used // (ncor * 16)) * 16
     count = sig.shape[0] * ncor * time * ntm
     cfg = (ncor, ntm, nc, t, rows, 1.0 / math.sqrt(count))
     hbm = pl.BlockSpec(memory_space=pltpu.HBM)
@@ -502,9 +499,11 @@
             pltpu.VMEM(sig.shape, BF16),
             pltpu.VMEM(sig.shape, BF16),
             pltpu.VMEM(sig.shape, BF16),
+            pltpu.VMEM(w.shape, F32),
             pltpu.VMEM(wb.shape, F32),
+            pltpu.VMEM(p.shape, F32),
             pltpu.VMEM(pb.shape, F32),
-            dma((9,)),
+            dma((7,)),
             field,
             field,
             field,
@@ -524,15 +523,16 @@
             pltpu.VMEM((2, po, 128), F32),
             pltpu.VMEM((2, g2, 256), F32),
             pltpu.VMEM((2, po, 256), F32),
-            pltpu.VMEM((2, ncor * rows, 128), F32),
-            pltpu.VMEM((2, ncor - 1, rows, 128), F32),
-            pltpu.VMEM((2, ntm, rows, 128), F32),
-            pltpu.VMEM((2, ncor * rows, 128), F32),
+            pltpu.VMEM((16, 128), F32),
+            pltpu.VMEM((ncor * rows, 128), BF16),
+            pltpu.VMEM((ncor - 1, rows, 128), BF16),
+            pltpu.VMEM((ntm, rows, 128), BF16),
+            pltpu.VMEM((ncor * rows, 128), BF16),
         ]
         + [dma((nc,))] * 8
-        + [dma((2, ncor - 1))] * 2
-        + [dma((2, ntm - 1))] * 2
-        + [dma((2, ncor - 1))] * 2,
+        + [dma((ncor - 1,))] * 2
+        + [dma((ntm - 1,))] * 2
+        + [dma((ncor - 1,))] * 2,
         compiler_params=pltpu.CompilerParams(
             collective_id=0, has_side_effects=True, vmem_limit_bytes=room
         ),
@@ -545,7 +545,7 @@
         out_shape=tuple(jax.ShapeDtypeStruct(a.shape, a.dtype) for a in outs),
         in_specs=[hbm] * 7,
         out_specs=[hbm] * 7,
-        scratch_shapes=[dma((7,))],
+        scratch_shapes=[pltpu.VMEM(a.shape, a.dtype) for a in outs] + [dma((2, 7))],
         compiler_params=pltpu.CompilerParams(vmem_limit_bytes=room),
     )(*outs)
 

time: 132 us -> 70.8 us (0.54)
  Pallas kernels: 131 us -> 69.9 us
    pallas_call x1, Pallas kernels: 60.8 us -> 2.43 us  [on_device(): pl.pallas_call(deliver, out_shape=tuple((jax.ShapeDtypeStruct(a.shape, a....]
    pallas_call x1, Pallas kernels: 70.6 us -> 67.5 us  [on_device(): pl.pallas_call(functools.partial(kernel, cfg), out_shape=(jax.ShapeDtypeS...]
where the time goes in v3:
time: 70.8 us; the launch traced here: 70.6 us
  Pallas kernels  69.9 us (99%)
    pallas_call x1, Pallas kernels, on_device(): pl.pallas_call(functools.partial(kernel, cfg), out_shape=(jax.ShapeDtypeS...  67.5 us
    pallas_call x1, Pallas kernels, on_device(): pl.pallas_call(deliver, out_shape=tuple((jax.ShapeDtypeStruct(a.shape, a....  2.43 us

profile of v3, /device:TPU:0, one launch (start us, length us, event | category | flops | bytes accessed | tf_op | source)
XLA Modules:
  0.0 70.6 jit_solution(10928260877424266515)
XLA Ops:
  0.6 67.5 %shard_map.126 = (bf16[1,64,4096]{2,1,0:T(8,128)(2,1)}, bf16[1,64,4096]{2,1,0:T(8,128)(2,1)}, bf16[1,64,4096]{2,1,0:T(8,128)(2,1)}, f32[2,256,128]{2,1,0:T(8,128...) custom-call(bf16[1,64,4096]{2,1,0:T(8,128)(2,1)} %sig_h.1, bf16[2,256,128]{2,1,0:T(8,128)(2,1)} %w_h.1, ...), custom_call_target="tpu_custom_call" | custom-call | flops 2415919104 | bytes 3145728 | tf_op jit(solution)/shard_map/pallas_call | solution.py:483
  68.1 2.4 %shard_map.127 = (bf16[1,64,4096]{2,1,0:T(8,128)(2,1)}, bf16[1,64,4096]{2,1,0:T(8,128)(2,1)}, bf16[1,64,4096]{2,1,0:T(8,128)(2,1)}, f32[2,256,128]{2,1,0:T(8,128...) custom-call(bf16[1,64,4096]{2,1,0:T(8,128)(2,1)} %get-tuple-element.14.refs_0_, ...), custom_call_target="tpu_custom_call" | custom-call | tf_op jit(solution)/shard_map/pallas_call | solution.py:543

commit v4 on v3

--- a/solution.py
+++ b/solution.py
@@ -12,7 +12,8 @@
 F32 = jnp.float32
 BF16 = jnp.bfloat16
 CHUNK = 512
-LAG = 2
+LAG_TOP = 1
+LAG_LOW = 3
 
 
 def dot(a, b):
@@ -74,6 +75,7 @@
     pbc,
     accw,
     accp,
+    accb,
     bias,
     part,
     rs_buf,
@@ -95,7 +97,6 @@
     ag_r,
 ):
     ncor, ntm, nc, t, rows, scale = cfg
-    lag = min(LAG, nc)
     r = sig.shape[1]
     g = p.shape[2]
     g2 = w.shape[1]
@@ -104,7 +105,7 @@
     zi = lax.axis_index("tm")
 
     def cols(i):
-        return pl.ds(pl.multiple_of(i * t, t), t)
+        return pl.ds(i * t if isinstance(i, int) else pl.multiple_of(i * t, t), t)
 
     def shift_copy(src, dst, ssem, rsem, i, distance):
         return pltpu.make_async_remote_copy(
@@ -163,6 +164,7 @@
         pbc[l] = jnp.broadcast_to(pb[l : l + 1, :], (128, po)).T
     accw[...] = jnp.zeros_like(accw)
     accp[...] = jnp.zeros_like(accp)
+    accb[...] = jnp.zeros_like(accb)
     part[...] = jnp.zeros_like(part)
     bias[...] = jnp.zeros_like(bias)
 
@@ -192,7 +194,12 @@
 
         lax.fori_loop(0, nc, send, 0)
 
-    ones = jnp.ones((128, t), BF16)
+    def fold(v):
+        v = v.astype(F32)
+        s = v[:, 0:128]
+        for k in range(1, t // 128):
+            s = s + v[:, k * 128 : (k + 1) * 128]
+        return s
 
     def wide(ref, l):
         return jnp.concatenate([ref[l]] * (t // 128), axis=1)
@@ -207,14 +214,22 @@
         return sg - z * th, z - z * sg, zb, mixed
 
     def accumulate(l, gpre, stacked, u, zb):
-        accw[l] += dot_nt(gpre, jnp.concatenate([stacked, ones], axis=0))
-        accp[l] += dot_nt(u, jnp.concatenate([zb, ones], axis=0))
-
-    def forward_low(i, carry):
+        accw[l] += dot_nt(gpre, stacked)
+        accp[l] += dot_nt(u, zb)
+        accb[l, 0:g2] += fold(gpre)
+        accb[l, g2 : g2 + po] += fold(u)
+
+    def wait_sig(i):
         @pl.when(zi >= 1)
         def _():
             sig_copy(i).wait_recv()
 
+    def send_x(i):
+        @pl.when(zi < ntm - 2)
+        def _():
+            x_copy(i).start()
+
+    def forward_low(i):
         a = sig[0, :, cols(i)]
         df, dg, zb, mixed = gates(0, jnp.concatenate([tap0[i], a], axis=0))
         xmid[i] = (a.astype(F32) + mixed[:r]).astype(BF16)
@@ -222,12 +237,6 @@
         dg0[i] = dg
         z0[i] = zb
         skip0[i] = mixed[r:]
-
-        @pl.when(zi < ntm - 2)
-        def _():
-            x_copy(i).start()
-
-        return carry
 
     def wait_x(i):
         @pl.when(zi >= 2)
@@ -275,26 +284,26 @@
         stacked = jnp.concatenate([tap0[i], sig[0, :, cols(i)]], axis=0)
         accumulate(0, gpre, stacked, u, z0[i])
 
-    def top_only(i, carry):
-        wait_x(i)
-        top(i)
-        send_d1(i)
-        return carry
-
-    def both(i, carry):
-        wait_x(i)
-        wait_d1(i - lag)
-        low(i - lag)
-        top(i)
-        send_d1(i)
-        send_d0(i - lag)
-        return carry
-
-    def low_only(i, carry):
-        wait_d1(i)
-        low(i)
-        send_d0(i)
-        return carry
+    def step(i, first, second, third):
+        j, k = i - LAG_TOP, i - LAG_LOW
+        if first:
+            wait_sig(i)
+        if second:
+            wait_x(j)
+        if third:
+            wait_d1(k)
+        if third:
+            low(k)
+        if first:
+            forward_low(i)
+        if second:
+            top(j)
+        if first:
+            send_x(i)
+        if second:
+            send_d1(j)
+        if third:
+            send_d0(k)
 
     def finish(i, carry):
         @pl.when(zi < ntm - 1)
@@ -351,14 +360,12 @@
     cuts = g2 // 128
 
     def fill(l):
-        part[l * mats : l * mats + g2] = accw[l, :, 0:128].astype(BF16)
-        part[l * mats + g2 : (l + 1) * mats] = accp[l, :, 0:128].astype(BF16)
-        brow = accw[l, :, 128:256].T
-        for k in range(cuts):
+        part[l * mats : l * mats + g2] = accw[l].astype(BF16)
+        part[l * mats + g2 : (l + 1) * mats] = accp[l].astype(BF16)
+        brow = jnp.sum(accb[l].T, axis=0, keepdims=True)
+        for k in range(cuts + 1):
             at = l * (cuts + 1) + k
-            bias[at : at + 1] = brow[0:1, k * 128 : (k + 1) * 128]
-        at = l * (cuts + 1) + cuts
-        bias[at : at + 1] = accp[l, :, 128:256].T[0:1, :]
+            bias[at : at + 1] = brow[:, k * 128 : (k + 1) * 128]
 
     def rs_start():
         part[2 * mats : 2 * mats + 16] = bias[...].astype(BF16)
@@ -392,13 +399,20 @@
             at = l * (cuts + 1) + cuts
             gobias[l : l + 1, :] = tail[at : at + 1]
 
-    lax.fori_loop(0, nc, forward_low, 0)
-    lax.fori_loop(0, lag, top_only, 0)
-    lax.fori_loop(lag, nc, both, 0)
+    def full(i, carry):
+        step(i, True, True, True)
+        return carry
+
+    for i in range(LAG_LOW):
+        step(i, True, i >= LAG_TOP, False)
+    lax.fori_loop(LAG_LOW, nc, full, 0)
+    for i in range(nc, nc + LAG_TOP):
+        step(i, False, True, True)
     put(xtop, xtop_h, 0).start()
     put(skip, skip_h, 1).start()
     fill(1)
-    lax.fori_loop(nc - lag, nc, low_only, 0)
+    for i in range(nc + LAG_TOP, nc + LAG_LOW):
+        step(i, False, False, True)
     fill(0)
     rs_start()
     z_start()
@@ -521,8 +535,9 @@
             pltpu.VMEM((2, g, po), BF16),
             pltpu.VMEM((2, g2, 128), F32),
             pltpu.VMEM((2, po, 128), F32),
-            pltpu.VMEM((2, g2, 256), F32),
-            pltpu.VMEM((2, po, 256), F32),
+            pltpu.VMEM((2, g2, w.shape[2]), F32),
+            pltpu.VMEM((2, po, g), F32),
+            pltpu.VMEM((2, g2 + po, 128), F32),
             pltpu.VMEM((16, 128), F32),
             pltpu.VMEM((ncor * rows, 128), BF16),
             pltpu.VMEM((ncor - 1, rows, 128), BF16),

time: 70.8 us -> 71.6 us (1.011)
  Pallas kernels: 69.9 us -> 70.8 us
    pallas_call x1, Pallas kernels: 67.5 us -> 68.4 us  [on_device(): pl.pallas_call(functools.partial(kernel, cfg), out_shape=(jax.ShapeDtypeS...]
where the time goes in v4:
time: 71.6 us; the launch traced here: 71.5 us
  Pallas kernels  70.8 us (99%)
    pallas_call x1, Pallas kernels, on_device(): pl.pallas_call(functools.partial(kernel, cfg), out_shape=(jax.ShapeDtypeS...  68.4 us
    pallas_call x1, Pallas kernels, on_device(): pl.pallas_call(deliver, out_shape=tuple((jax.ShapeDtypeStruct(a.shape, a....  2.43 us

profile of v4, /device:TPU:0, one launch (start us, length us, event | category | flops | bytes accessed | tf_op | source)
XLA Modules:
  0.0 71.5 jit_solution(4509946551219109321)
XLA Ops:
  0.6 68.4 %shard_map.126 = (bf16[1,64,4096]{2,1,0:T(8,128)(2,1)}, bf16[1,64,4096]{2,1,0:T(8,128)(2,1)}, bf16[1,64,4096]{2,1,0:T(8,128)(2,1)}, f32[2,256,128]{2,1,0:T(8,128...) custom-call(bf16[1,64,4096]{2,1,0:T(8,128)(2,1)} %sig_h.1, bf16[2,256,128]{2,1,0:T(8,128)(2,1)} %w_h.1, ...), custom_call_target="tpu_custom_call" | custom-call | flops 2415919104 | bytes 3145728 | tf_op jit(solution)/shard_map/pallas_call | solution.py:497
  69.0 2.4 %shard_map.127 = (bf16[1,64,4096]{2,1,0:T(8,128)(2,1)}, bf16[1,64,4096]{2,1,0:T(8,128)(2,1)}, bf16[1,64,4096]{2,1,0:T(8,128)(2,1)}, f32[2,256,128]{2,1,0:T(8,128...) custom-call(bf16[1,64,4096]{2,1,0:T(8,128)(2,1)} %get-tuple-element.14.refs_0_, ...), custom_call_target="tpu_custom_call" | custom-call | tf_op jit(solution)/shard_map/pallas_call | solution.py:558

commit v5 on v4

--- a/solution.py
+++ b/solution.py
@@ -13,7 +13,8 @@
 BF16 = jnp.bfloat16
 CHUNK = 512
 LAG_TOP = 1
-LAG_LOW = 3
+LAG_LOW = 2
+AHEAD = 2
 
 
 def dot(a, b):
@@ -186,13 +187,13 @@
 
     pl.semaphore_wait(barrier, ncor - 1 + ntm - 1)
 
-    @pl.when(zi < ntm - 1)
-    def _():
-        def send(i, carry):
+    def send_sig(i):
+        @pl.when(zi < ntm - 1)
+        def _():
             sig_copy(i).start()
-            return carry
-
-        lax.fori_loop(0, nc, send, 0)
+
+    for i in range(AHEAD):
+        send_sig(i)
 
     def fold(v):
         v = v.astype(F32)
@@ -288,21 +289,23 @@
         j, k = i - LAG_TOP, i - LAG_LOW
         if first:
             wait_sig(i)
+            forward_low(i)
+            send_x(i)
+            if not isinstance(i, int):
+
+                @pl.when(i + AHEAD < nc)
+                def _():
+                    send_sig(i + AHEAD)
+
+            elif i + AHEAD < nc:
+                send_sig(i + AHEAD)
         if second:
             wait_x(j)
+            top(j)
+            send_d1(j)
         if third:
             wait_d1(k)
-        if third:
             low(k)
-        if first:
-            forward_low(i)
-        if second:
-            top(j)
-        if first:
-            send_x(i)
-        if second:
-            send_d1(j)
-        if third:
             send_d0(k)
 
     def finish(i, carry):

time: 71.6 us -> 64.4 us (0.90)
  Pallas kernels: 70.8 us -> 63.3 us
    pallas_call x1, Pallas kernels: 68.4 us -> 60.8 us  [on_device(): pl.pallas_call(functools.partial(kernel, cfg), out_shape=(jax.ShapeDtypeS...]
where the time goes in v5:
time: 64.4 us; the launch traced here: 63.9 us
  Pallas kernels  63.3 us (98%)
    pallas_call x1, Pallas kernels, on_device(): pl.pallas_call(functools.partial(kernel, cfg), out_shape=(jax.ShapeDtypeS...  60.8 us
    pallas_call x1, Pallas kernels, on_device(): pl.pallas_call(deliver, out_shape=tuple((jax.ShapeDtypeStruct(a.shape, a....  2.43 us

profile of v5, /device:TPU:0, one launch (start us, length us, event | category | flops | bytes accessed | tf_op | source)
XLA Modules:
  0.0 63.9 jit_solution(9771735762577219494)
XLA Ops:
  0.6 60.8 %shard_map.126 = (bf16[1,64,4096]{2,1,0:T(8,128)(2,1)}, bf16[1,64,4096]{2,1,0:T(8,128)(2,1)}, bf16[1,64,4096]{2,1,0:T(8,128)(2,1)}, f32[2,256,128]{2,1,0:T(8,128...) custom-call(bf16[1,64,4096]{2,1,0:T(8,128)(2,1)} %sig_h.1, bf16[2,256,128]{2,1,0:T(8,128)(2,1)} %w_h.1, ...), custom_call_target="tpu_custom_call" | custom-call | flops 2415919104 | bytes 3145728 | tf_op jit(solution)/shard_map/pallas_call | solution.py:500
  61.5 2.4 %shard_map.127 = (bf16[1,64,4096]{2,1,0:T(8,128)(2,1)}, bf16[1,64,4096]{2,1,0:T(8,128)(2,1)}, bf16[1,64,4096]{2,1,0:T(8,128)(2,1)}, f32[2,256,128]{2,1,0:T(8,128...) custom-call(bf16[1,64,4096]{2,1,0:T(8,128)(2,1)} %get-tuple-element.14.refs_0_, ...), custom_call_target="tpu_custom_call" | custom-call | tf_op jit(solution)/shard_map/pallas_call | solution.py:561

commit v6 on v5

--- a/solution.py
+++ b/solution.py
@@ -11,10 +11,10 @@
 MESH = pl.DeviceIdType.MESH
 F32 = jnp.float32
 BF16 = jnp.bfloat16
-CHUNK = 512
-LAG_TOP = 1
-LAG_LOW = 2
-AHEAD = 2
+CHUNK = 256
+LAG_TOP = 2
+LAG_LOW = 6
+AHEAD = 3
 
 
 def dot(a, b):
@@ -402,20 +402,21 @@
             at = l * (cuts + 1) + cuts
             gobias[l : l + 1, :] = tail[at : at + 1]
 
-    def full(i, carry):
-        step(i, True, True, True)
-        return carry
-
-    for i in range(LAG_LOW):
-        step(i, True, i >= LAG_TOP, False)
-    lax.fori_loop(LAG_LOW, nc, full, 0)
-    for i in range(nc, nc + LAG_TOP):
-        step(i, False, True, True)
+    def steps(lo, hi, first, second, third):
+        def body(i, carry):
+            step(i, first, second, third)
+            return carry
+
+        lax.fori_loop(lo, hi, body, 0)
+
+    steps(0, LAG_TOP, True, False, False)
+    steps(LAG_TOP, LAG_LOW, True, True, False)
+    steps(LAG_LOW, nc, True, True, True)
+    steps(nc, nc + LAG_TOP, False, True, True)
     put(xtop, xtop_h, 0).start()
     put(skip, skip_h, 1).start()
     fill(1)
-    for i in range(nc + LAG_TOP, nc + LAG_LOW):
-        step(i, False, False, True)
+    steps(nc + LAG_TOP, nc + LAG_LOW, False, False, True)
     fill(0)
     rs_start()
     z_start()

time: 64.4 us -> 66.3 us (1.030); the launches traced: 63.9 us -> 65.1 us
  Pallas kernels: 63.3 us -> 64.5 us
    pallas_call x1, Pallas kernels: 60.8 us -> 62.1 us  [on_device(): pl.pallas_call(functools.partial(kernel, cfg), out_shape=(jax.ShapeDtypeS...]
where the time goes in v6:
time: 66.3 us; the launch traced here: 65.1 us
  Pallas kernels  64.5 us (97%)
    pallas_call x1, Pallas kernels, on_device(): pl.pallas_call(functools.partial(kernel, cfg), out_shape=(jax.ShapeDtypeS...  62.1 us
    pallas_call x1, Pallas kernels, on_device(): pl.pallas_call(deliver, out_shape=tuple((jax.ShapeDtypeStruct(a.shape, a....  2.43 us

profile of v6, /device:TPU:0, one launch (start us, length us, event | category | flops | bytes accessed | tf_op | source)
XLA Modules:
  0.0 65.1 jit_solution(2992966123209342275)
XLA Ops:
  0.6 62.1 %shard_map.126 = (bf16[1,64,4096]{2,1,0:T(8,128)(2,1)}, bf16[1,64,4096]{2,1,0:T(8,128)(2,1)}, bf16[1,64,4096]{2,1,0:T(8,128)(2,1)}, f32[2,256,128]{2,1,0:T(8,128...) custom-call(bf16[1,64,4096]{2,1,0:T(8,128)(2,1)} %sig_h.1, bf16[2,256,128]{2,1,0:T(8,128)(2,1)} %w_h.1, ...), custom_call_target="tpu_custom_call" | custom-call | flops 2415919104 | bytes 3145728 | tf_op jit(solution)/shard_map/pallas_call | solution.py:501
  62.7 2.4 %shard_map.127 = (bf16[1,64,4096]{2,1,0:T(8,128)(2,1)}, bf16[1,64,4096]{2,1,0:T(8,128)(2,1)}, bf16[1,64,4096]{2,1,0:T(8,128)(2,1)}, f32[2,256,128]{2,1,0:T(8,128...) custom-call(bf16[1,64,4096]{2,1,0:T(8,128)(2,1)} %get-tuple-element.14.refs_0_, ...), custom_call_target="tpu_custom_call" | custom-call | tf_op jit(solution)/shard_map/pallas_call | solution.py:562

commit v7 on v5

--- a/solution.py
+++ b/solution.py
@@ -13,7 +13,7 @@
 BF16 = jnp.bfloat16
 CHUNK = 512
 LAG_TOP = 1
-LAG_LOW = 2
+LAG_LOW = 3
 AHEAD = 2
 
 

time: 64.4 us -> 67.6 us (1.050); the launches traced: 63.9 us -> 66.4 us
  Pallas kernels: 63.3 us -> 65.7 us
    pallas_call x1, Pallas kernels: 60.8 us -> 63.3 us  [on_device(): pl.pallas_call(functools.partial(kernel, cfg), out_shape=(jax.ShapeDtypeS...]
where the time goes in v7:
time: 67.6 us; the launch traced here: 66.4 us
  Pallas kernels  65.7 us (97%)
    pallas_call x1, Pallas kernels, on_device(): pl.pallas_call(functools.partial(kernel, cfg), out_shape=(jax.ShapeDtypeS...  63.3 us
    pallas_call x1, Pallas kernels, on_device(): pl.pallas_call(deliver, out_shape=tuple((jax.ShapeDtypeStruct(a.shape, a....  2.43 us

profile of v7, /device:TPU:0, one launch (start us, length us, event | category | flops | bytes accessed | tf_op | source)
XLA Modules:
  0.0 66.4 jit_solution(13480127291749402357)
XLA Ops:
  0.6 63.3 %shard_map.126 = (bf16[1,64,4096]{2,1,0:T(8,128)(2,1)}, bf16[1,64,4096]{2,1,0:T(8,128)(2,1)}, bf16[1,64,4096]{2,1,0:T(8,128)(2,1)}, f32[2,256,128]{2,1,0:T(8,128...) custom-call(bf16[1,64,4096]{2,1,0:T(8,128)(2,1)} %sig_h.1, bf16[2,256,128]{2,1,0:T(8,128)(2,1)} %w_h.1, ...), custom_call_target="tpu_custom_call" | custom-call | flops 2415919104 | bytes 3145728 | tf_op jit(solution)/shard_map/pallas_call | solution.py:500
  63.9 2.4 %shard_map.127 = (bf16[1,64,4096]{2,1,0:T(8,128)(2,1)}, bf16[1,64,4096]{2,1,0:T(8,128)(2,1)}, bf16[1,64,4096]{2,1,0:T(8,128)(2,1)}, f32[2,256,128]{2,1,0:T(8,128...) custom-call(bf16[1,64,4096]{2,1,0:T(8,128)(2,1)} %get-tuple-element.14.refs_0_, ...), custom_call_target="tpu_custom_call" | custom-call | tf_op jit(solution)/shard_map/pallas_call | solution.py:561
